TPU v7x, 32 devices: a whole 2x2x4 slice. The times are simulated.
32 devices in a mesh: grp: 2 (over x), wide: 8 (over z, y), narrow: 2 (over core).
Axes of the slice: x: 2, y: 2, z: 4, core: 2. Of those that a mesh axis runs over, the one named last changes fastest.
Arguments:
- tokens: bfloat16 [10240, 8192], P(('grp', 'wide'), 'narrow'), parts along dimension 0, may hold values from -6 to 6
- key_value_weight: bfloat16 [8192, 2048], P('narrow'), may hold values from -0.0625 to 0.0625
- adapter_down_weight: bfloat16 [8192, 64, 64], P('narrow', ('grp', 'wide')), parts along dimension 1, may hold values from -0.0625 to 0.0625
- adapter_up_weight: bfloat16 [64, 64, 2048], P(('grp', 'wide')), parts along dimension 0, may hold values from -0.75 to 0.75
- token_adapter_index: int32 [10240], P(('grp', 'wide')), parts along dimension 0, may hold values from 0 to 31, as said below
- adapter_rank_list: int32 [64], P(('grp', 'wide')), parts along dimension 0, may hold values from 16 to 64, as said below
Outputs:
- projected: bfloat16 [10240, 2048], P(('grp', 'wide'), 'narrow'), parts along dimension 0
There are 2 independent parts, one for each index of `grp`. A program takes and returns all parts, laid end to end along the dimension named above; an argument that names none is the same for every part. Nothing has to cross between parts.
Inputs may be any that keep to these rules, and one draw needn't show every extreme that they name: `token_adapter_index`: tokens of one index of wide come in pieces of 16 that share an adapter. The adapters a with a // 4 = o belong to owner o; at most 128 tokens of one index of wide name adapters of one owner, and in every draw some owner gets exactly 128 tokens from every index of wide. `adapter_rank_list`: each rank is 64, 32 or 16.
All inputs are finite; a program needn't handle non-finite values.
Results may differ from a plain program's by a relative error of at most 0.006.
Values may be sent and summed in bfloat16 or wider, within the bound.
A program may use at most 192 MiB of HBM per device.

v0:
```python
import jax
import jax.numpy as jnp
from jax import lax
from jax.sharding import PartitionSpec as P

ALPHA = 32
BLOCK = 128
PIECE = 16


def local(
    tokens,
    key_value_weight,
    adapter_down_weight,
    adapter_up_weight,
    token_adapter_index,
    adapter_rank_list,
):
    wide_count = lax.axis_size("wide")
    wide_index = lax.axis_index("wide")
    local_count = adapter_rank_list.shape[0]
    rank_limit = adapter_down_weight.shape[2]
    width_halved = tokens.shape[1]
    column_indices = local_count * rank_limit
    owner_of = token_adapter_index // local_count
    owner_onehot = (owner_of[:, None] == jnp.arange(wide_count, dtype=jnp.int32)[None, :]).astype(
        jnp.int32
    )
    position = jnp.sum((jnp.cumsum(owner_onehot, axis=0) - 1) * owner_onehot, axis=1)
    slot_index = owner_of * BLOCK + position
    send_rows = (
        jnp.zeros((wide_count * BLOCK, width_halved), jnp.bfloat16).at[slot_index].set(tokens)
    )
    send_rows = send_rows.reshape(wide_count, BLOCK, width_halved)
    send_ident = (
        jnp.full((wide_count * BLOCK,), -1, jnp.int32).at[slot_index].set(token_adapter_index)
    )
    send_ident = send_ident.reshape(wide_count, BLOCK)
    flattened_down = adapter_down_weight.reshape(width_halved, column_indices)
    column_adapter = jnp.arange(column_indices, dtype=jnp.int32) // rank_limit
    column_rank = jnp.arange(column_indices, dtype=jnp.int32) % rank_limit
    rank_of_column = jnp.repeat(adapter_rank_list, rank_limit, total_repeat_length=column_indices)
    column_scale = jnp.where(
        column_rank < rank_of_column, ALPHA / rank_of_column.astype(jnp.float32), jnp.float32(0.0)
    )
    arrived = lax.all_to_all(send_rows, "wide", split_axis=0, concat_axis=0, tiled=True)
    arrived_ident = lax.all_to_all(send_ident, "wide", split_axis=0, concat_axis=0, tiled=True)
    local_identity = arrived_ident - wide_index * local_count
    partial_shrink = jnp.einsum(
        "wbd,dc->wbc", arrived, flattened_down, preferred_element_type=jnp.float32
    )
    coefficient = jnp.where(
        local_identity[:, :, None] == column_adapter[None, None, :],
        column_scale[None, None, :],
        jnp.float32(0.0),
    )
    source_count = partial_shrink.shape[0]
    block_row_list = partial_shrink.shape[1]
    scaled = (partial_shrink * coefficient).reshape(
        source_count, block_row_list, local_count, rank_limit
    )
    chosen_rows = jnp.sum(scaled, axis=2)
    piece_rows = block_row_list // PIECE

    def single_up_weight(source):
        source_scaled, source_ident = source
        portion_adapter = jnp.clip(
            source_ident.reshape(piece_rows, PIECE)[:, 0], 0, local_count - 1
        )
        portion_up_weight = jnp.take(adapter_up_weight, portion_adapter, axis=0)
        grouped = source_scaled.reshape(piece_rows, PIECE, rank_limit)
        leading = grouped.astype(jnp.bfloat16)
        remainder = (grouped - leading.astype(jnp.float32)).astype(jnp.bfloat16)
        result = jnp.einsum(
            "pqr,prk->pqk", leading, portion_up_weight, preferred_element_type=jnp.float32
        )
        result = result + jnp.einsum(
            "pqr,prk->pqk", remainder, portion_up_weight, preferred_element_type=jnp.float32
        )
        return result.reshape(block_row_list, portion_up_weight.shape[2])

    adapter_owned_rows = lax.map(single_up_weight, (chosen_rows, local_identity))
    gathered_back = lax.all_to_all(
        adapter_owned_rows, "wide", split_axis=0, concat_axis=0, tiled=True
    )
    adapter_correction = jnp.take(
        gathered_back.reshape(wide_count * BLOCK, gathered_back.shape[2]), slot_index, axis=0
    )
    base_projected_part = jnp.dot(tokens, key_value_weight, preferred_element_type=jnp.float32)
    projected = lax.psum_scatter(
        base_projected_part + adapter_correction, "narrow", scatter_dimension=1, tiled=True
    ).astype(jnp.bfloat16)
    return projected


def solution(mesh):
    in_specs = (
        P(("grp", "wide"), "narrow"),
        P("narrow", None),
        P("narrow", ("grp", "wide"), None),
        P(("grp", "wide"), None, None),
        P(("grp", "wide")),
        P(("grp", "wide")),
    )
    out_specs = P(("grp", "wide"), "narrow")
    return jax.shard_map(local, mesh=mesh, in_specs=in_specs, out_specs=out_specs, check_vma=False)
```

profile of v0, /device:TPU:1, one launch (start us, length us, event | category | flops | bytes accessed | tf_op | source)
XLA Modules:
  0.0 500.8 jit_solution(17955541313673439056)
XLA Ops:
  6.5 0.8 add_select_fusion
  7.4 1.4 reduce-window.14
  9.4 0.7 compare_and_fusion
  10.1 4.8 scatter_custom_fusion.1
  14.9 6.4 %all-to-all-start.1 = ((s32[8,1,128]{2,1,0:T(1,128)}), s32[8,1,128]{2,1,0:T(1,128)S(1)}, u32[]{:S(2)}, u32[]{:S(2)}) async-start(s32[8,1,128]{2,1,0:T(1,128)} %bitcast.9), calls=%async_computation.1 | async-start | bytes 8192 | tf_op jit(solution)/shard_map/all_to_all | solution.py:47
  21.3 17.8 %scatter_custom_fusion = bf16[1024,4096]{1,0:T(8,128)(2,1)} fusion(s32[640]{0:T(1024)S(1)} %get-tuple-element.61, bf16[640,4096]{1,0:T(8,128)(2,1)} %param.10, bf16[]{:T(256)} %constant.187.clone.1), kind=kCustom, calls=%fused_computation.21 | custom fusion | bytes 8389120 | tf_op jit(solution)/shard_map/scatter | solution.py:32
  39.1 5.6 %all-to-all-start = ((bf16[8,128,4096]{2,1,0:T(8,128)(2,1)}), bf16[8,128,4096]{2,1,0:T(8,128)(2,1)}, u32[]{:S(2)}, u32[]{:S(2)}) async-start(bf16[8,128,4096]{2,1,0:T(8,128)(2,1)} %bitcast.49), calls=%async_computation | async-start | bytes 16777216 | tf_op jit(solution)/shard_map/all_to_all | solution.py:46
  45.4 2.4 compare_select_fusion.3
  47.9 178.5 %all-to-all-done = bf16[8,128,4096]{2,1,0:T(8,128)(2,1)} async-done(((bf16[8,128,4096]{2,1,0:T(8,128)(2,1)}), bf16[8,128,4096]{2,1,0:T(8,128)(2,1)}, u32[]{:S(2)}, u32[]{:S(2)}) %all-to-all-start) | async-done | bytes 8388640 | tf_op jit(solution)/shard_map/all_to_all | solution.py:46
  226.4 6.8 %convolution_multiply_fusion = f32[8,128,256]{2,1,0:T(8,128)} fusion(bf16[8,128,4096]{2,1,0:T(8,128)(2,1)} %all-to-all-done, bf16[4096,256,1]{0,1,2:T(8,128)(2,1)S(1)} %bitcast.47, f32[256]{0:T(256)S(1)} %compare_select_fusion.7, s32[256]{0:T(256)S(1)} %and_select_fusion.2, s32[8,128]{1,0:T(8,128)S(1)} %bitcast.59), kind=kOutput, calls=%fused_computation.23 | convolution fusion | flops 2148270080 | bytes 11540480 | tf_op jit(solution)/shard_map/wbd,dc->wbc/dot_general | solution.py:49
  233.2 1.5 copy.17
  234.8 25.7 %while.11 = (s32[]{:T(128)}, f32[8,128,2048]{2,1,0:T(8,128)}, f32[8,128,64]{1,2,0:T(8,128)S(1)}, s32[8,128]{1,0:T(8,128)S(1)}, bf16[4,64,2048]{2,1,0:T(8,128)(2,1)S(1)}, /*index=5*/s32[]{:T(128)}) while((s32[]{:T(128)}, f32[8,128,2048]{2,1,0:T(8,128)}, f32[8,128,64]{1,2,0:T(8,128)S(1)}, s32[8,128]{1,0:T(8,128)S(1)}, ...), condition=%wide.region_7.8_spmd, body=%wide.region_6.7_spmd.sunk | while | flops 69510232 | bytes 13835013 | solution.py:82
  235.1 0.7 gather_fusion
  237.0 1.1 bitcast_dynamic-update-slice_fusion.2
  240.2 1.1 bitcast_dynamic-update-slice_fusion.2
  241.5 0.7 gather_fusion
  243.4 1.1 bitcast_dynamic-update-slice_fusion.2
  244.7 0.7 gather_fusion
  246.6 1.1 bitcast_dynamic-update-slice_fusion.2
  247.9 0.7 gather_fusion
  249.8 1.1 bitcast_dynamic-update-slice_fusion.2
  251.1 0.7 gather_fusion
  253.0 1.1 bitcast_dynamic-update-slice_fusion.2
  254.4 0.7 gather_fusion
  256.2 1.1 bitcast_dynamic-update-slice_fusion.2
  259.5 1.1 bitcast_dynamic-update-slice_fusion.2
  260.5 5.3 %all-to-all-start.2 = ((f32[8,128,2048]{2,1,0:T(8,128)}), f32[8,128,2048]{2,1,0:T(8,128)}, u32[]{:S(2)}, u32[]{:S(2)}) async-start(f32[8,128,2048]{2,1,0:T(8,128)} %get-tuple-element.44), calls=%async_computation.2 | async-start | bytes 16777216 | tf_op jit(solution)/shard_map/all_to_all | solution.py:83
  265.9 181.1 %all-to-all-done.2 = f32[8,128,2048]{2,1,0:T(8,128)} async-done(((f32[8,128,2048]{2,1,0:T(8,128)}), f32[8,128,2048]{2,1,0:T(8,128)}, u32[]{:S(2)}, u32[]{:S(2)}) %all-to-all-start.2) | async-done | bytes 8388640 | tf_op jit(solution)/shard_map/all_to_all | solution.py:83
  447.0 10.2 %gather_fusion.1 = f32[640,2048]{1,0:T(8,128)} fusion(f32[1024,2048]{1,0:T(8,128)} %bitcast.21, s32[1024]{0:T(1024)S(1)} %pad_clamp_fusion.1), kind=kCustom, calls=%fused_computation.1 | custom fusion | bytes 10488320 | tf_op jit(solution)/shard_map/jit(_take)/gather | solution.py:86
  457.2 18.5 %select_add_fusion = f32[640,2048]{1,0:T(8,128)} fusion(f32[640,2048]{1,0:T(8,128)} %gather_fusion.1, bf16[640,4096]{1,0:T(8,128)(2,1)} %param.10, bf16[4096,2048]{1,0:T(8,128)(2,1)} %param.11, pred[640]{0:T(1024)(128)(4,1)S(1)} %get-tuple-element.60), kind=kOutput, calls=%fused_computation.20 | convolution fusion | flops 10740039680 | bytes 32506496 | tf_op jit(solution)/shard_map/dot_general | solution.py:89
  475.7 15.3 %reduce-scatter.2.cloned.1.call-done = f32[640,1024]{1,0:T(8,128)} async-done(((f32[640,2048]{1,0:T(8,128)}), f32[640,1024]{1,0:T(8,128)}) %reduce-scatter.2.cloned.1.call-update) | async-done | bytes 2621456 | tf_op jit(solution)/shard_map/reduce_scatter | solution.py:90
  490.9 3.0 convert_element_type.26
  (102 shorter events, 14.1 us)
Async XLA Ops:
  6.5 219.8 %copy-start = (bf16[4096,4,64]{0,2,1:T(8,128)(2,1)S(1)}, bf16[4096,4,64]{0,2,1:T(8,128)(2,1)}, u32[]{:S(2)}) copy-start(bf16[4096,4,64]{0,2,1:T(8,128)(2,1)} %param.12) | copy-start | bytes 6291460
  14.9 24.2 %all-to-all-start.1 = ((s32[8,1,128]{2,1,0:T(1,128)}), s32[8,1,128]{2,1,0:T(1,128)S(1)}, u32[]{:S(2)}, u32[]{:S(2)}) async-start(s32[8,1,128]{2,1,0:T(1,128)} %bitcast.9), calls=%async_computation.1 | async-start | bytes 8192 | tf_op jit(solution)/shard_map/all_to_all | solution.py:47
  39.1 5.6 %copy-start.3 = (s32[4]{0:T(128)S(1)}, s32[4]{0:T(128)}, u32[]{:S(2)}) copy-start(s32[4]{0:T(128)} %param.15) | copy-start | bytes 52
  39.1 6.2 %copy-start.4 = (s32[2,128]{1,0:T(2,128)S(1)}, s32[2,128]{1,0:T(2,128)}, u32[]{:S(2)}) copy-start(s32[2,128]{1,0:T(2,128)} %constant.194.clone.1) | copy-start | bytes 3076
  39.1 187.3 %all-to-all-start = ((bf16[8,128,4096]{2,1,0:T(8,128)(2,1)}), bf16[8,128,4096]{2,1,0:T(8,128)(2,1)}, u32[]{:S(2)}, u32[]{:S(2)}) async-start(bf16[8,128,4096]{2,1,0:T(8,128)(2,1)} %bitcast.49), calls=%async_computation | async-start | bytes 16777216 | tf_op jit(solution)/shard_map/all_to_all | solution.py:46
  226.4 8.5 %copy-start.2 = (bf16[4,64,2048]{2,1,0:T(8,128)(2,1)S(1)}, bf16[4,64,2048]{2,1,0:T(8,128)(2,1)}, u32[]{:S(2)}) copy-start(bf16[4,64,2048]{2,1,0:T(8,128)(2,1)} %param.13) | copy-start | bytes 3145732
  260.5 186.4 %all-to-all-start.2 = ((f32[8,128,2048]{2,1,0:T(8,128)}), f32[8,128,2048]{2,1,0:T(8,128)}, u32[]{:S(2)}, u32[]{:S(2)}) async-start(f32[8,128,2048]{2,1,0:T(8,128)} %get-tuple-element.44), calls=%async_computation.2 | async-start | bytes 16777216 | tf_op jit(solution)/shard_map/all_to_all | solution.py:83
  265.8 225.1 %reduce-scatter.2.cloned.1.call-start = ((), (), s32[]{:S(2)}) async-start(), calls=%async_computation.4 | async-start | bytes 7864320 | tf_op jit(solution)/shard_map/reduce_scatter | solution.py:90
  457.2 36.7 %copy-start.1 = (bf16[4096,4,64]{0,2,1:T(8,128)(2,1)S(1)}, bf16[4096,4,64]{0,2,1:T(8,128)(2,1)}, u32[]{:S(2)}) copy-start(bf16[4096,4,64]{0,2,1:T(8,128)(2,1)} %param.12) | copy-start | bytes 6291460
Sparse Core Ops, SparseCore 0:
  475.8 15.0 reduce-scatter.1
where the time goes:
time: 501 us
  waiting for transfers between devices  375 us (75%)
  local copies, waits for them, and re-layouts  51.1 us (10%)
  matrix products  32.9 us (7%)
  starting transfers between devices  17.2 us (3%)
  between operations  13.5 us (3%)
  other arithmetic  10.9 us (2%)
    all_to_all x1, waiting for transfers between devices, local(): lax.all_to_all(adapter_owned_rows, 'wide', split_axis=0, concat_axis=0, t...  181 us
    all_to_all x1, waiting for transfers between devices, local(): lax.all_to_all(send_rows, 'wide', split_axis=0, concat_axis=0, tiled=True)  178 us
    dot_general x1, matrix products, local(): jnp.dot(tokens, key_value_weight, preferred_element_type=jnp.float32)  18.5 us
    scatter x1, local copies, waits for them, and re-layouts, local(): jnp.zeros((wide_count * BLOCK, width_halved), jnp.bfloat16).at[slot_index]  17.8 us
    reduce_scatter x1, waiting for transfers between devices, local(): lax.psum_scatter(base_projected_part + adapter_correction, 'narrow', scat...  15.3 us
    gather x1, local copies, waits for them, and re-layouts, local(): jnp.take(gathered_back.reshape(wide_count * BLOCK, gathered_back.shape[2]...  10.2 us
  transfers between devices with their start and end apart: 4, of which 3 were waited for; matrix products, arithmetic and copies ran while one was open for 4% of the time, Pallas kernels for 0%

commit v1 on v0

v1 whole, which is shorter than its diff:
```python
import jax
import jax.numpy as jnp
from jax import lax
from jax.sharding import PartitionSpec as P

ALPHA = 32


def local(
    tokens,
    key_value_weight,
    adapter_down_weight,
    adapter_up_weight,
    token_adapter_index,
    adapter_rank_list,
):
    narrow_count = lax.axis_size("narrow")
    narrow_index = lax.axis_index("narrow")
    rows, depth = tokens.shape
    local_count, rank_limit, width = adapter_up_weight.shape
    columns = local_count * rank_limit
    part = width // narrow_count
    down = adapter_down_weight.reshape(depth, columns)
    up = lax.dynamic_slice_in_dim(
        adapter_up_weight.reshape(columns, width), narrow_index * part, part, 1
    )
    all_down = lax.all_gather(down, "wide")
    all_up = lax.all_gather(up, "wide", tiled=True)
    all_rank = lax.all_gather(adapter_rank_list, "wide", tiled=True)
    adapters = all_rank.shape[0]

    base = jnp.dot(tokens, key_value_weight, preferred_element_type=jnp.float32)
    base = lax.psum_scatter(base, "narrow", scatter_dimension=1, tiled=True)

    same = token_adapter_index[:, None] == jnp.arange(adapters, dtype=jnp.int32)[None, :]
    shrink = jnp.einsum("td,wdc->twc", tokens, all_down, preferred_element_type=jnp.float32)
    shrink = shrink.reshape(rows, adapters, rank_limit)
    chosen = jnp.sum(jnp.where(same[:, :, None], shrink, jnp.float32(0.0)), axis=1)
    chosen = lax.psum(chosen, "narrow")
    rank = jnp.sum(jnp.where(same, all_rank[None, :], 0), axis=1)
    kept = jnp.arange(rank_limit, dtype=jnp.int32)[None, :] < rank[:, None]
    scaled = jnp.where(kept, chosen * (ALPHA / rank.astype(jnp.float32))[:, None], jnp.float32(0.0))
    spread = jnp.where(same[:, :, None], scaled[:, None, :], jnp.float32(0.0)).astype(jnp.bfloat16)
    adapted = jnp.dot(
        spread.reshape(rows, adapters * rank_limit), all_up, preferred_element_type=jnp.float32
    )
    return (base + adapted).astype(jnp.bfloat16)


def solution(mesh):
    in_specs = (
        P(("grp", "wide"), "narrow"),
        P("narrow", None),
        P("narrow", ("grp", "wide"), None),
        P(("grp", "wide"), None, None),
        P(("grp", "wide")),
        P(("grp", "wide")),
    )
    out_specs = P(("grp", "wide"), "narrow")
    return jax.shard_map(local, mesh=mesh, in_specs=in_specs, out_specs=out_specs, check_vma=False)
```

time: 501 us -> 381 us (0.76)
  waiting for transfers between devices: 375 us -> 306 us
  local copies, waits for them, and re-layouts: 51.1 us -> 6.49 us
  starting transfers between devices: 17.2 us -> 0.13 us
  matrix products: 32.9 us -> 43 us
  blocking collectives: 0 us -> 7.16 us
  other arithmetic: 10.9 us -> 4.49 us
    all_to_all x3 -> x0, waiting for transfers between devices: 360 us -> none  [the longest x1 181 us: local(): lax.all_to_all(adapter_owned_rows, 'wide', split_axis=0, concat_axis=0, t...]
    all_gather x0 -> x2, waiting for transfers between devices: none -> 290 us  [the longest x1 229 us: local(): all_down = lax.all_gather(down, 'wide')]
    scatter x2 -> x0, local copies, waits for them, and re-layouts: 22.6 us -> none  [the longest x1 17.8 us: local(): jnp.zeros((wide_count * BLOCK, width_halved), jnp.bfloat16).at[slot_index]]
    all_to_all x3 -> x0, starting transfers between devices: 17.2 us -> none  [the longest x1 6.38 us: local(): lax.all_to_all(send_ident, 'wide', split_axis=0, concat_axis=0, tiled=True)]
    gather x10 -> x0, local copies, waits for them, and re-layouts: 16.3 us -> none  [the longest x1 10.2 us: local(): jnp.take(gathered_back.reshape(wide_count * BLOCK, gathered_back.shape[2]...]
    dot_general x18 -> x3, matrix products: 32.9 us -> 43 us  [the longest x1 17.7 us: local(): jnp.einsum('td,wdc->twc', tokens, all_down, preferred_element_type=jnp.fl...]
    dynamic_update_slice x8 -> x0, local copies, waits for them, and re-layouts: 8.75 us -> none  [local(): lax.map(single_up_weight, (chosen_rows, local_identity))]
    unnamed x0 -> x1, blocking collectives: none -> 7.16 us
  transfers between devices with their start and end apart: 4 -> 4, of which waited for: 3 -> 3; matrix products, arithmetic and copies ran while one was open for 4% -> 6% of each run, Pallas kernels for 0% -> 0%
where the time goes in v1:
time: 381 us
  waiting for transfers between devices  306 us (80%)
  matrix products  43 us (11%)
  between operations  13.8 us (4%)
  blocking collectives  7.16 us (2%)
  local copies, waits for them, and re-layouts  6.49 us (2%)
  other arithmetic  4.49 us (1%)
    all_gather x1, waiting for transfers between devices, local(): all_down = lax.all_gather(down, 'wide')  229 us
    all_gather x1, waiting for transfers between devices, local(): all_up = lax.all_gather(up, 'wide', tiled=True)  61.1 us
    dot_general x1, matrix products, local(): jnp.einsum('td,wdc->twc', tokens, all_down, preferred_element_type=jnp.fl...  17.7 us
    dot_general x1, matrix products, local(): base = jnp.dot(tokens, key_value_weight, preferred_element_type=jnp.float32)  17.6 us
    reduce_scatter x1, waiting for transfers between devices, local(): base = lax.psum_scatter(base, 'narrow', scatter_dimension=1, tiled=True)  15.3 us
    dot_general x1, matrix products, local(): jnp.dot(spread.reshape(rows, adapters * rank_limit), all_up, preferred_el...  7.73 us
  transfers between devices with their start and end apart: 4, of which 3 were waited for; matrix products, arithmetic and copies ran while one was open for 6% of the time, Pallas kernels for 0%

profile of v1, /device:TPU:1, one launch (start us, length us, event | category | flops | bytes accessed | tf_op | source)
XLA Modules:
  0.0 381.0 jit_solution(9228414796879926106)
XLA Ops:
  6.5 0.0 copy-start
  6.5 0.0 copy-start.1
  6.5 0.0 all-gather.3.cloned.1.call-start
  6.5 4.2 %copy.9 = bf16[1,4096,256]{2,1,0:T(8,128)(2,1)} copy(bf16[1,4096,256]{1,2,0:T(8,128)(2,1)} %bitcast.16) | data formatting | bytes 4194304 | tf_op jit(solution)/shard_map/all_gather;reshape | solution.py:27
  10.7 0.0 all-gather.3.cloned.1.call-update
  10.8 0.0 all-reduce.3.cloned.1.call-start
  10.8 0.0 copy-done.1
  10.8 229.4 %all-gather.3.cloned.1.call-done = bf16[8,4096,256]{2,1,0:T(8,128)(2,1)} async-done(((bf16[1,4096,256]{2,1,0:T(8,128)(2,1)}), bf16[8,4096,256]{2,1,0:T(8,128)(2,1)}) %all-gather.3.cloned.1.call-update) | async-done | bytes 16777232 | tf_op jit(solution)/shard_map/all_gather | solution.py:27
  240.2 17.7 %fusion = f32[640,8,256]{0,2,1:T(8,128)S(1)} fusion(bf16[8,4096,256]{2,1,0:T(8,128)(2,1)} %all-gather.3.cloned.1.call-done, bf16[640,4096]{1,0:T(8,128)(2,1)} %param.6), kind=kOutput, calls=%fused_computation | convolution fusion | flops 10737418240 | bytes 27262976 | tf_op jit(solution)/shard_map/td,wdc->twc/dot_general | solution.py:36
  257.9 1.3 select_reduce_fusion
  259.1 0.0 all-reduce.3.cloned.1.call-update
  259.1 0.0 all-gather.5.cloned.1.call-start
  259.2 0.0 copy-done
  259.2 0.8 constant_dynamic-slice_fusion
  260.0 0.0 all-gather.5.cloned.1.call-update
  260.1 0.0 reduce-scatter.2.cloned.1.call-start
  260.1 17.6 %fusion.2 = f32[640,2048]{1,0:T(8,128)} fusion(bf16[640,4096]{1,0:T(8,128)(2,1)} %param.6, bf16[4096,2048]{1,0:T(8,128)(2,1)} %param.7), kind=kOutput, calls=%fused_computation.11 | convolution fusion | flops 10737418240 | bytes 27262976 | tf_op jit(solution)/shard_map/dot_general | solution.py:32
  277.8 0.0 copy-start.3
  277.8 0.0 copy-start.2
  277.8 0.0 reduce-scatter.2.cloned.1.call-update
  277.8 0.6 copy-done.3
  278.4 0.6 dynamic-slice
  279.6 0.0 copy-done.2
  279.6 0.2 dynamic-update-slice
  279.9 7.2 %all-reduce = s32[32]{0:T(128)S(1)} all-reduce(s32[32]{0:T(128)S(1)} %dynamic-update-slice), channel_id=1, replica_groups=mesh['grp'=2,'wide'=8,'narrow'=2] {'wide'}, use_global_device_ids=true, to_apply=%add | all-reduce | flops 32 | bytes 256
  287.0 0.1 select_reduce_fusion.1
  287.2 0.0 all-reduce.3.cloned.1.call-done
  287.2 1.0 multiply_select_fusion
  288.1 2.2 select_convert_fusion
  290.3 61.1 %all-gather.5.cloned.1.call-done = bf16[2048,1024]{1,0:T(8,128)(2,1)} async-done(((bf16[256,1024]{1,0:T(8,128)(2,1)}), bf16[2048,1024]{1,0:T(8,128)(2,1)}) %all-gather.5.cloned.1.call-update) | async-done | bytes 4194320 | tf_op jit(solution)/shard_map/all_gather | solution.py:28
  351.4 15.3 %reduce-scatter.2.cloned.1.call-done = f32[640,1024]{1,0:T(8,128)} async-done(((f32[640,2048]{1,0:T(8,128)}), f32[640,1024]{1,0:T(8,128)}) %reduce-scatter.2.cloned.1.call-update) | async-done | bytes 2621456 | tf_op jit(solution)/shard_map/reduce_scatter | solution.py:33
  366.7 7.7 %add_convert_fusion = bf16[640,1024]{1,0:T(8,128)(2,1)} fusion(f32[640,1024]{1,0:T(8,128)} %reduce-scatter.2.cloned.1.call-done, bf16[640,2048]{0,1:T(8,128)(2,1)} %bitcast.15, bf16[2048,1024]{1,0:T(8,128)(2,1)} %all-gather.5.cloned.1.call-done), kind=kOutput, calls=%fused_computation.4 | convolution fusion | flops 2685665280 | bytes 10747904 | tf_op jit(solution)/shard_map/dot_general | solution.py:44
  (3 shorter events, 0.0 us)
Async XLA Ops:
  6.5 252.7 %copy-start = (bf16[4,64,2048]{2,1,0:T(8,128)(2,1)S(1)}, bf16[4,64,2048]{2,1,0:T(8,128)(2,1)}, u32[]{:S(2)}) copy-start(bf16[4,64,2048]{2,1,0:T(8,128)(2,1)} %param.9) | copy-start | bytes 3145732
  6.5 4.3 %copy-start.1 = (s32[640]{0:T(1024)S(1)}, s32[640]{0:T(1024)}, u32[]{:S(2)}) copy-start(s32[640]{0:T(1024)} %param.10) | copy-start | bytes 7684
  6.5 233.7 %all-gather.3.cloned.1.call-start = ((), (), s32[]{:S(2)}) async-start(), calls=%async_computation.2 | async-start | bytes 18874368 | tf_op jit(solution)/shard_map/all_gather | solution.py:27
  10.8 276.4 %all-reduce.3.cloned.1.call-start = ((), (), s32[]{:S(2)}) async-start(), calls=%async_computation.3 | async-start | bytes 327680 | tf_op jit(solution)/shard_map/psum | solution.py:39
  259.1 92.3 %all-gather.5.cloned.1.call-start = ((), (), s32[]{:S(2)}) async-start(), calls=%async_computation.4 | async-start | bytes 4718592 | tf_op jit(solution)/shard_map/all_gather | solution.py:28
  260.1 106.7 %reduce-scatter.2.cloned.1.call-start = ((), (), s32[]{:S(2)}) async-start(), calls=%async_computation.1 | async-start | bytes 7864320 | tf_op jit(solution)/shard_map/reduce_scatter | solution.py:33
  277.8 0.7 copy-start.3
  277.8 1.9 copy-start.2
Sparse Core Ops, SparseCore 0:
  10.9 229.2 all-gather.2
  259.3 16.9 all-reduce.2
  278.4 73.0 all-gather.4
  353.6 13.0 reduce-scatter.1

commit v2 on v1

v2 whole, which is shorter than its diff:
```python
import functools

import jax
import jax.numpy as jnp
from jax import lax
from jax.experimental import pallas as pl
from jax.experimental.pallas import tpu as pltpu
from jax.sharding import PartitionSpec as P

ALPHA = 32
MESH = pl.DeviceIdType.MESH
FIRST = 3


def chunks_of(slabs):
    main = slabs - FIRST
    size = main // 4
    ranges = [(FIRST + i * size, size if i < 3 else main - 3 * size) for i in range(4)]
    return ranges + [(0, FIRST)]


def kernel(
    wide_count,
    tokens_ref,
    weight_ref,
    block_ref,
    code_ref,
    out_ref,
    buf,
    tok,
    tile,
    part,
    got,
    upv,
    total,
    total_got,
    spread,
    tok_sem,
    tile_sem,
    up_sem,
    z_send,
    z_recv,
    y_send,
    y_recv,
    own_send,
    own_recv,
    n_send,
    n_recv,
):
    planes = wide_count // 2
    me = lax.axis_index("wide")
    core = lax.axis_index("narrow")
    z = me // 2
    y = me % 2
    partner = z * 2 + (1 - y)
    other = 1 - core
    slabs = block_ref.shape[0]
    depth_slabs = weight_ref.shape[0]
    slab = weight_ref.shape[1]
    tiles = weight_ref.shape[2] // slab
    half = tiles // 2
    chunks = chunks_of(slabs)
    main_count = len(chunks) - 1

    barrier = pltpu.get_barrier_semaphore()
    pl.semaphore_signal(barrier, inc=1, device_id={"wide": partner}, device_id_type=MESH)
    pl.semaphore_signal(barrier, inc=1, device_id={"narrow": other}, device_id_type=MESH)

    @pl.when(z > 0)
    def _():
        pl.semaphore_signal(barrier, inc=1, device_id={"wide": me - 2}, device_id_type=MESH)

    @pl.when(z < planes - 1)
    def _():
        pl.semaphore_signal(barrier, inc=1, device_id={"wide": me + 2}, device_id_type=MESH)

    peers = 2 + jnp.where(z > 0, 1, 0) + jnp.where(z < planes - 1, 1, 0)
    pl.semaphore_wait(barrier, peers)

    def z_copy(way, step, chunk, owner_z):
        if chunk < len(chunks):
            start, size = chunks[chunk]
            owner = owner_z * 2 + y
            source = block_ref if step == 1 else buf.at[owner]
        else:
            start, size = chunks[-1]
            owner = owner_z * 2 + (1 - y)
            source = buf.at[owner]
        return pltpu.make_async_remote_copy(
            src_ref=source.at[pl.ds(start, size)],
            dst_ref=buf.at[owner, pl.ds(start, size)],
            send_sem=z_send.at[way, step - 1, chunk],
            recv_sem=z_recv.at[way, step - 1, chunk],
            device_id={"wide": me + 2 if way == 0 else me - 2},
            device_id_type=MESH,
        )

    def y_copy(way, step, chunk, owner):
        start, size = chunks[chunk]
        return pltpu.make_async_remote_copy(
            src_ref=buf.at[owner, pl.ds(start, size)],
            dst_ref=buf.at[owner, pl.ds(start, size)],
            send_sem=y_send.at[way, step - 1, chunk],
            recv_sem=y_recv.at[way, step - 1, chunk],
            device_id={"wide": partner},
            device_id_type=MESH,
        )

    def own_copy(which, owner):
        start, size = (0, FIRST) if which == 0 else (FIRST, slabs - FIRST)
        return pltpu.make_async_remote_copy(
            src_ref=block_ref.at[pl.ds(start, size)],
            dst_ref=buf.at[owner, pl.ds(start, size)],
            send_sem=own_send.at[which],
            recv_sem=own_recv.at[which],
            device_id={"wide": partner},
            device_id_type=MESH,
        )

    def n_copy(source, target, which):
        return pltpu.make_async_remote_copy(
            src_ref=source,
            dst_ref=target,
            send_sem=n_send.at[which],
            recv_sem=n_recv.at[which],
            device_id={"narrow": other},
            device_id_type=MESH,
        )

    def can_send(way):
        return z < planes - 1 if way == 0 else z > 0

    def arrives(way, step):
        return z >= step if way == 0 else z + step <= planes - 1

    def forwards(way, step):
        return jnp.logical_and(arrives(way, step), can_send(way))

    def plane_of(way, step):
        return z - step if way == 0 else z + step

    load_tokens = pltpu.make_async_copy(tokens_ref, tok, tok_sem)
    load_tokens.start()
    own_copy(0, me).start()
    for chunk in range(len(chunks)):
        for way in range(2):

            @pl.when(can_send(way))
            def _(way=way, chunk=chunk):
                z_copy(way, 1, chunk, z).start()

    own_copy(1, me).start()
    own_copy(0, partner).wait_recv()
    for way in range(2):

        @pl.when(can_send(way))
        def _(way=way):
            z_copy(way, 1, len(chunks), z).start()

    def weight_load(step, slot):
        column = jnp.where(step < half, other * half + step, core * half + step - half)
        return pltpu.make_async_copy(
            weight_ref.at[:, :, pl.ds(pl.multiple_of(column * slab, slab), slab)],
            tile.at[slot],
            tile_sem.at[slot],
        )

    def product(slot):
        value = None
        group = 4
        def body(k, carry):
            offset = pl.multiple_of(k * (group * slab), group * slab)
            left = tok[:, pl.ds(offset, group * slab)]
            right = tile[slot, pl.ds(k * group, group)].reshape(group * slab, slab)
            return carry + jnp.dot(left, right, preferred_element_type=jnp.float32)

        zero = jnp.zeros((tok.shape[0], slab), jnp.float32)
        return lax.fori_loop(0, depth_slabs // group, body, zero)

    weight_load(0, 0).start()
    load_tokens.wait()

    def base_step(step, carry):
        slot = step % 2

        @pl.when(step < tiles - 1)
        def _():
            weight_load(step + 1, 1 - slot).start()

        weight_load(step, slot).wait()
        part[step] = product(slot)

        return carry

    lax.fori_loop(0, tiles, base_step, 0)
    base_copy = n_copy(part.at[pl.ds(0, half)], got, 0)
    base_copy.start()

    total[...] = jnp.zeros_like(total)

    def shrink(source, owner):
        down = pltpu.make_async_copy(source.at[pl.ds(0, depth_slabs)], tile.at[0], tile_sem.at[0])
        up = pltpu.make_async_copy(
            source.at[pl.ds(depth_slabs, slabs - depth_slabs)], upv.at[:, owner], up_sem
        )
        down.start()
        up.start()
        down.wait()
        up.wait()
        total[...] += jnp.where(code_ref[...] == owner, product(0), jnp.float32(0.0))

    shrink(block_ref, me)

    def across(step):
        for way in range(2):

            @pl.when(arrives(way, step))
            def _(way=way):
                owner = plane_of(way, step) * 2 + (1 - y)
                for chunk in range(main_count):
                    y_copy(way, step, chunk, owner).wait_recv()
                shrink(buf.at[owner], owner)

    for step in range(1, planes):
        for chunk in range(len(chunks) + 1):
            for way in range(2):

                @pl.when(arrives(way, step))
                def _(way=way, chunk=chunk):
                    plane = plane_of(way, step)
                    z_copy(way, step, chunk, plane).wait_recv()
                    if chunk < main_count:
                        y_copy(way, step, chunk, plane * 2 + y).start()

                if step < planes - 1:

                    @pl.when(forwards(way, step))
                    def _(way=way, chunk=chunk):
                        z_copy(way, step + 1, chunk, plane_of(way, step)).start()

        for way in range(2):

            @pl.when(arrives(way, step))
            def _(way=way):
                owner = plane_of(way, step) * 2 + y
                shrink(buf.at[owner], owner)

        if step == 1:
            own_copy(1, partner).wait_recv()
            shrink(buf.at[partner], partner)
        else:
            across(step - 1)
    across(planes - 1)

    total_copy = n_copy(total, total_got, 1)
    total_copy.start()
    total_copy.wait_recv()
    whole = total[...] + total_got[...]
    for owner in range(wide_count):
        spread[:, owner * slab : (owner + 1) * slab] = jnp.where(
            code_ref[...] == owner, whole, jnp.float32(0.0)
        ).astype(jnp.bfloat16)
    base_copy.wait_recv()

    def finish(i, carry):
        right = upv[i].reshape(wide_count * slab, slab)
        adapted = jnp.dot(spread[...], right, preferred_element_type=jnp.float32)
        value = part[half + i] + got[i] + adapted
        out_ref[:, pl.ds(pl.multiple_of(i * slab, slab), slab)] = value.astype(jnp.bfloat16)
        return carry

    lax.fori_loop(0, half, finish, 0)

    base_copy.wait_send()
    total_copy.wait_send()
    for which in range(2):
        own_copy(which, me).wait_send()
    for step in range(1, planes):
        for way in range(2):
            sends = can_send(way) if step == 1 else forwards(way, step - 1)

            @pl.when(sends)
            def _(way=way, step=step):
                for chunk in range(len(chunks) + 1):
                    z_copy(way, step, chunk, plane_of(way, step - 1)).wait_send()

            @pl.when(arrives(way, step))
            def _(way=way, step=step):
                for chunk in range(main_count):
                    y_copy(way, step, chunk, plane_of(way, step) * 2 + y).wait_send()


def local(
    tokens,
    key_value_weight,
    adapter_down_weight,
    adapter_up_weight,
    token_adapter_index,
    adapter_rank_list,
):
    wide_count = lax.axis_size("wide")
    narrow_count = lax.axis_size("narrow")
    narrow_index = lax.axis_index("narrow")
    rows, depth = tokens.shape
    local_count, rank_limit, width = adapter_up_weight.shape
    columns = local_count * rank_limit
    part = width // narrow_count
    depth_slabs = depth // columns
    part_slabs = part // columns
    slabs = depth_slabs + part_slabs
    planes = wide_count // 2

    up = lax.dynamic_slice_in_dim(adapter_up_weight, narrow_index * part, part, 2)
    rank = adapter_rank_list[:, None]
    kept = jnp.arange(rank_limit, dtype=jnp.int32)[None, :] < rank
    scale = jnp.where(kept, ALPHA / rank.astype(jnp.float32), jnp.float32(0.0))
    up = (up.astype(jnp.float32) * scale[:, :, None]).astype(jnp.bfloat16)
    up = up.reshape(columns, part_slabs, columns).transpose(1, 0, 2)
    block = jnp.concatenate([adapter_down_weight.reshape(depth_slabs, columns, columns), up], axis=0)
    column_adapter = jnp.arange(columns, dtype=jnp.int32) // rank_limit
    code = jnp.where(
        (token_adapter_index % local_count)[:, None] == column_adapter[None, :],
        (token_adapter_index // local_count)[:, None],
        -1,
    )

    any_space = pl.BlockSpec(memory_space=pl.ANY)
    vmem = pl.BlockSpec(memory_space=pltpu.VMEM)
    dma = pltpu.SemaphoreType.DMA
    out, _ = pl.pallas_call(
        functools.partial(kernel, wide_count),
        out_shape=(
            jax.ShapeDtypeStruct((rows, part), jnp.bfloat16),
            jax.ShapeDtypeStruct((wide_count, slabs, columns, columns), jnp.bfloat16),
        ),
        in_specs=[any_space, any_space, any_space, vmem],
        out_specs=(vmem, any_space),
        scratch_shapes=[
            pltpu.VMEM((rows, depth), jnp.bfloat16),
            pltpu.VMEM((2, depth_slabs, columns, columns), jnp.bfloat16),
            pltpu.VMEM((2 * part_slabs, rows, columns), jnp.float32),
            pltpu.VMEM((part_slabs, rows, columns), jnp.float32),
            pltpu.VMEM((part_slabs, wide_count, columns, columns), jnp.bfloat16),
            pltpu.VMEM((rows, columns), jnp.float32),
            pltpu.VMEM((rows, columns), jnp.float32),
            pltpu.VMEM((rows, wide_count * columns), jnp.bfloat16),
            dma,
            dma((2,)),
            dma,
            dma((2, planes - 1, 6)),
            dma((2, planes - 1, 6)),
            dma((2, planes - 1, 4)),
            dma((2, planes - 1, 4)),
            dma((2,)),
            dma((2,)),
            dma((2,)),
            dma((2,)),
        ],
        compiler_params=pltpu.CompilerParams(
            collective_id=0, has_side_effects=True, vmem_limit_bytes=56 * 1024 * 1024
        ),
    )(tokens, key_value_weight.reshape(depth_slabs, columns, width), block, code)
    return out


def solution(mesh):
    in_specs = (
        P(("grp", "wide"), "narrow"),
        P("narrow", None),
        P("narrow", ("grp", "wide"), None),
        P(("grp", "wide"), None, None),
        P(("grp", "wide")),
        P(("grp", "wide")),
    )
    out_specs = P(("grp", "wide"), "narrow")
    return jax.shard_map(local, mesh=mesh, in_specs=in_specs, out_specs=out_specs, check_vma=False)
```

time: 381 us -> 235 us (0.62)
  waiting for transfers between devices: 306 us -> 0 us
  Pallas kernels: 0 us -> 221 us
  matrix products: 43 us -> 0 us
  between operations: 13.8 us -> 0.04 us
  blocking collectives: 7.16 us -> 0 us
    all_gather x2 -> x0, waiting for transfers between devices: 290 us -> none  [the longest x1 229 us: local(): all_down = lax.all_gather(down, 'wide')]
    pallas_call x0 -> x1, Pallas kernels: none -> 221 us  [local(): pl.pallas_call(functools.partial(kernel, wide_count), out_shape=(jax.Shap...]
    dot_general x3 -> x0, matrix products: 43 us -> none  [the longest x1 17.7 us: local(): jnp.einsum('td,wdc->twc', tokens, all_down, preferred_element_type=jnp.fl...]
    reduce_scatter x1 -> x0, waiting for transfers between devices: 15.3 us -> none  [local(): base = lax.psum_scatter(base, 'narrow', scatter_dimension=1, tiled=True)]
    unnamed x1 -> x0, blocking collectives: 7.16 us -> none
    another operation x1 -> x0, local copies, waits for them, and re-layouts: 4.19 us -> none  [local(): all_down = lax.all_gather(down, 'wide')]
  transfers between devices with their start and end apart: 4 -> 0, of which waited for: 3 -> 0; matrix products, arithmetic and copies ran while one was open for 6% -> 0% of each run, Pallas kernels for 0% -> 0%
where the time goes in v2:
time: 235 us
  Pallas kernels  221 us (94%)
  local copies, waits for them, and re-layouts  7.9 us (3%)
  other arithmetic  6.26 us (3%)
    pallas_call x1, Pallas kernels, local(): pl.pallas_call(functools.partial(kernel, wide_count), out_shape=(jax.Shap...  221 us

profile of v2, /device:TPU:1, one launch (start us, length us, event | category | flops | bytes accessed | tf_op | source)
XLA Modules:
  0.0 234.7 jit_solution(13566328863205991193)
XLA Ops:
  0.0 0.0 copy-start
  0.0 0.8 convert_divide_fusion
  0.8 0.7 fusion.2
  1.5 0.7 add_select_fusion.1
  2.2 1.2 multiply_convert_fusion
  3.4 0.4 reshape.65
  3.8 0.1 copy.12
  3.9 1.1 compare_select_fusion.code_ref
  5.0 0.0 copy-done
  5.0 2.0 copy.10
  7.0 3.0 %copy.9 = bf16[16,256,256]{2,1,0:T(8,128)(2,1)S(1)} copy(bf16[16,256,256]{1,0,2:T(8,128)(2,1)} %bitcast.10) | data formatting | bytes 4194304 | tf_op jit(solution)/shard_map/reshape | solution.py:319
  10.0 1.8 pad_maximum_fusion.block_ref
  11.7 220.5 %shard_map.64 = (bf16[640,1024]{1,0:T(8,128)(2,1)}, bf16[8,20,256,256]{3,2,1,0:T(8,128)(2,1)}) custom-call(bf16[640,4096]{1,0:T(8,128)(2,1)} %tokens_ref.1, bf16[16,256,2048]{2,1,0:T(8,128)(2,1)} %bitcast.9, bf16[20,256,256]{2,1,0:T(8,128)(2,1)} %pad_maximum_fusion.block_ref, s32[640,256]{1,0:T(8,128)} %compare_select_fusion.code_ref), custom_call_target="tpu_custom_call" | custom-call | tf_op jit(solution)/shard_map/pallas_call | solution.py:330
  232.2 2.5 %copy.14 = bf16[640,1024]{1,0:T(8,128)(2,1)} copy(bf16[640,1024]{1,0:T(8,128)(2,1)} %get-tuple-element.6) | data formatting | bytes 2621440
  (1 shorter events, 0.0 us)
Async XLA Ops:
  0.0 5.0 %copy-start = (bf16[4096,4,64]{0,2,1:T(8,128)(2,1)S(1)}, bf16[4096,4,64]{0,2,1:T(8,128)(2,1)}, u32[]{:S(2)}) copy-start(bf16[4096,4,64]{0,2,1:T(8,128)(2,1)} %param.8) | copy-start | bytes 6291460

commit v3 on v2

--- a/solution.py
+++ b/solution.py
@@ -12,23 +12,25 @@
 FIRST = 3
 
 
-def chunks_of(slabs):
-    main = slabs - FIRST
-    size = main // 4
-    ranges = [(FIRST + i * size, size if i < 3 else main - 3 * size) for i in range(4)]
-    return ranges + [(0, FIRST)]
+def chunks_of(down_slabs, slabs):
+    main = down_slabs - FIRST
+    size = main // 3
+    ranges = [(FIRST + i * size, size if i < 2 else main - 2 * size) for i in range(3)]
+    return ranges + [(down_slabs, slabs - down_slabs), (0, FIRST)]
 
 
 def kernel(
     wide_count,
     tokens_ref,
     weight_ref,
-    block_ref,
+    down_ref,
+    up_ref,
     code_ref,
     out_ref,
     buf,
     tok,
     tile,
+    down_tile,
     part,
     got,
     upv,
@@ -54,13 +56,21 @@
     y = me % 2
     partner = z * 2 + (1 - y)
     other = 1 - core
-    slabs = block_ref.shape[0]
+    down_slabs = down_ref.shape[0]
+    slabs = down_slabs + up_ref.shape[0]
     depth_slabs = weight_ref.shape[0]
+    depth = down_ref.shape[2]
     slab = weight_ref.shape[1]
     tiles = weight_ref.shape[2] // slab
     half = tiles // 2
-    chunks = chunks_of(slabs)
+    chunks = chunks_of(down_slabs, slabs)
     main_count = len(chunks) - 1
+
+    def mine(start, size):
+        if start < down_slabs:
+            return down_ref.at[pl.ds(start, size)]
+        return up_ref.at[pl.ds(start - down_slabs, size)]
+
 
     barrier = pltpu.get_barrier_semaphore()
     pl.semaphore_signal(barrier, inc=1, device_id={"wide": partner}, device_id_type=MESH)
@@ -81,13 +91,13 @@
         if chunk < len(chunks):
             start, size = chunks[chunk]
             owner = owner_z * 2 + y
-            source = block_ref if step == 1 else buf.at[owner]
+            source = mine(start, size) if step == 1 else buf.at[owner, pl.ds(start, size)]
         else:
             start, size = chunks[-1]
             owner = owner_z * 2 + (1 - y)
-            source = buf.at[owner]
+            source = buf.at[owner, pl.ds(start, size)]
         return pltpu.make_async_remote_copy(
-            src_ref=source.at[pl.ds(start, size)],
+            src_ref=source,
             dst_ref=buf.at[owner, pl.ds(start, size)],
             send_sem=z_send.at[way, step - 1, chunk],
             recv_sem=z_recv.at[way, step - 1, chunk],
@@ -107,9 +117,13 @@
         )
 
     def own_copy(which, owner):
-        start, size = (0, FIRST) if which == 0 else (FIRST, slabs - FIRST)
+        start, size = (
+            (0, FIRST),
+            (FIRST, down_slabs - FIRST),
+            (down_slabs, slabs - down_slabs),
+        )[which]
         return pltpu.make_async_remote_copy(
-            src_ref=block_ref.at[pl.ds(start, size)],
+            src_ref=mine(start, size),
             dst_ref=buf.at[owner, pl.ds(start, size)],
             send_sem=own_send.at[which],
             recv_sem=own_recv.at[which],
@@ -150,6 +164,7 @@
                 z_copy(way, 1, chunk, z).start()
 
     own_copy(1, me).start()
+    own_copy(2, me).start()
     own_copy(0, partner).wait_recv()
     for way in range(2):
 
@@ -198,18 +213,46 @@
 
     total[...] = jnp.zeros_like(total)
 
-    def shrink(source, owner):
-        down = pltpu.make_async_copy(source.at[pl.ds(0, depth_slabs)], tile.at[0], tile_sem.at[0])
-        up = pltpu.make_async_copy(
-            source.at[pl.ds(depth_slabs, slabs - depth_slabs)], upv.at[:, owner], up_sem
-        )
+    def down_product():
+        size = depth // 4
+
+        def body(k, carry):
+            offset = pl.multiple_of(k * size, size)
+            left = tok[:, pl.ds(offset, size)]
+            right = down_tile[:, :, pl.ds(offset, size)].reshape(slab, size)
+            return carry + lax.dot_general(
+                left, right, (((1,), (1,)), ((), ())), preferred_element_type=jnp.float32
+            )
+
+        zero = jnp.zeros((tok.shape[0], slab), jnp.float32)
+        return lax.fori_loop(0, 4, body, zero)
+
+    def shrink(down_source, up_source, owner):
+        groups = upv.shape[1]
+        width = upv.shape[4]
+        down = pltpu.make_async_copy(down_source, down_tile, tile_sem.at[0])
         down.start()
-        up.start()
+        ups = [
+            pltpu.make_async_copy(
+                up_source.at[:, :, pl.ds(g * width, width)], upv.at[owner, g], up_sem.at[g]
+            )
+            for g in range(groups)
+        ]
+        for up in ups:
+            up.start()
         down.wait()
-        up.wait()
-        total[...] += jnp.where(code_ref[...] == owner, product(0), jnp.float32(0.0))
-
-    shrink(block_ref, me)
+        total[...] += jnp.where(code_ref[...] == owner, down_product(), jnp.float32(0.0))
+        for up in ups:
+            up.wait()
+
+    shrink(down_ref, up_ref, me)
+
+    def arrived(owner):
+        shrink(
+            buf.at[owner, pl.ds(0, down_slabs)],
+            buf.at[owner, pl.ds(down_slabs, slabs - down_slabs)],
+            owner,
+        )
 
     def across(step):
         for way in range(2):
@@ -219,7 +262,7 @@
                 owner = plane_of(way, step) * 2 + (1 - y)
                 for chunk in range(main_count):
                     y_copy(way, step, chunk, owner).wait_recv()
-                shrink(buf.at[owner], owner)
+                arrived(owner)
 
     for step in range(1, planes):
         for chunk in range(len(chunks) + 1):
@@ -243,11 +286,12 @@
             @pl.when(arrives(way, step))
             def _(way=way):
                 owner = plane_of(way, step) * 2 + y
-                shrink(buf.at[owner], owner)
+                arrived(owner)
 
         if step == 1:
             own_copy(1, partner).wait_recv()
-            shrink(buf.at[partner], partner)
+            own_copy(2, partner).wait_recv()
+            arrived(partner)
         else:
             across(step - 1)
     across(planes - 1)
@@ -263,17 +307,18 @@
     base_copy.wait_recv()
 
     def finish(i, carry):
-        right = upv[i].reshape(wide_count * slab, slab)
+        columns = pl.ds(pl.multiple_of(i * slab, slab), slab)
+        right = upv[:, :, :, :, columns].reshape(wide_count * slab, slab)
         adapted = jnp.dot(spread[...], right, preferred_element_type=jnp.float32)
         value = part[half + i] + got[i] + adapted
-        out_ref[:, pl.ds(pl.multiple_of(i * slab, slab), slab)] = value.astype(jnp.bfloat16)
+        out_ref[:, columns] = value.astype(jnp.bfloat16)
         return carry
 
     lax.fori_loop(0, half, finish, 0)
 
     base_copy.wait_send()
     total_copy.wait_send()
-    for which in range(2):
+    for which in range(3):
         own_copy(which, me).wait_send()
     for step in range(1, planes):
         for way in range(2):
@@ -307,7 +352,12 @@
     part = width // narrow_count
     depth_slabs = depth // columns
     part_slabs = part // columns
-    slabs = depth_slabs + part_slabs
+    sub = 16
+    down_slabs = columns // sub
+    groups = depth // part
+    up_rows = columns // groups
+    up_slabs = up_rows // sub
+    slabs = down_slabs + up_slabs
     planes = wide_count // 2
 
     up = lax.dynamic_slice_in_dim(adapter_up_weight, narrow_index * part, part, 2)
@@ -315,8 +365,8 @@
     kept = jnp.arange(rank_limit, dtype=jnp.int32)[None, :] < rank
     scale = jnp.where(kept, ALPHA / rank.astype(jnp.float32), jnp.float32(0.0))
     up = (up.astype(jnp.float32) * scale[:, :, None]).astype(jnp.bfloat16)
-    up = up.reshape(columns, part_slabs, columns).transpose(1, 0, 2)
-    block = jnp.concatenate([adapter_down_weight.reshape(depth_slabs, columns, columns), up], axis=0)
+    up = up.reshape(groups, up_rows, part).transpose(1, 0, 2).reshape(up_slabs, sub, depth)
+    down = adapter_down_weight.transpose(1, 2, 0).reshape(down_slabs, sub, depth)
     column_adapter = jnp.arange(columns, dtype=jnp.int32) // rank_limit
     code = jnp.where(
         (token_adapter_index % local_count)[:, None] == column_adapter[None, :],
@@ -331,35 +381,36 @@
         functools.partial(kernel, wide_count),
         out_shape=(
             jax.ShapeDtypeStruct((rows, part), jnp.bfloat16),
-            jax.ShapeDtypeStruct((wide_count, slabs, columns, columns), jnp.bfloat16),
+            jax.ShapeDtypeStruct((wide_count, slabs, sub, depth), jnp.bfloat16),
         ),
-        in_specs=[any_space, any_space, any_space, vmem],
+        in_specs=[any_space, any_space, any_space, any_space, vmem],
         out_specs=(vmem, any_space),
         scratch_shapes=[
             pltpu.VMEM((rows, depth), jnp.bfloat16),
             pltpu.VMEM((2, depth_slabs, columns, columns), jnp.bfloat16),
+            pltpu.VMEM((down_slabs, sub, depth), jnp.bfloat16),
             pltpu.VMEM((2 * part_slabs, rows, columns), jnp.float32),
             pltpu.VMEM((part_slabs, rows, columns), jnp.float32),
-            pltpu.VMEM((part_slabs, wide_count, columns, columns), jnp.bfloat16),
+            pltpu.VMEM((wide_count, groups, up_slabs, sub, part), jnp.bfloat16),
             pltpu.VMEM((rows, columns), jnp.float32),
             pltpu.VMEM((rows, columns), jnp.float32),
             pltpu.VMEM((rows, wide_count * columns), jnp.bfloat16),
             dma,
             dma((2,)),
-            dma,
+            dma((groups,)),
             dma((2, planes - 1, 6)),
             dma((2, planes - 1, 6)),
             dma((2, planes - 1, 4)),
             dma((2, planes - 1, 4)),
-            dma((2,)),
-            dma((2,)),
+            dma((3,)),
+            dma((3,)),
             dma((2,)),
             dma((2,)),
         ],
         compiler_params=pltpu.CompilerParams(
             collective_id=0, has_side_effects=True, vmem_limit_bytes=56 * 1024 * 1024
         ),
-    )(tokens, key_value_weight.reshape(depth_slabs, columns, width), block, code)
+    )(tokens, key_value_weight.reshape(depth_slabs, columns, width), down, up, code)
     return out
 
 

time: 235 us -> 231 us (0.983)
  local copies, waits for them, and re-layouts: 7.9 us -> 4.09 us
where the time goes in v3:
time: 231 us; the launch traced here: 230 us
  Pallas kernels  222 us (96%)
  other arithmetic  4.35 us (2%)
  local copies, waits for them, and re-layouts  4.09 us (2%)
    pallas_call x1, Pallas kernels, local(): pl.pallas_call(functools.partial(kernel, wide_count), out_shape=(jax.Shap...  222 us

profile of v3, /device:TPU:1, one launch (start us, length us, event | category | flops | bytes accessed | tf_op | source)
XLA Modules:
  0.0 230.0 jit_solution(17794370928794130044)
XLA Ops:
  0.0 0.7 convert_divide_fusion
  0.7 0.7 fusion.3
  1.4 0.7 add_select_fusion.1
  2.1 1.2 fusion
  3.3 0.4 copy.7
  3.7 1.2 reshape.65.up_ref
  4.9 1.1 compare_select_fusion.code_ref
  6.0 221.5 %shard_map.64 = (bf16[640,1024]{1,0:T(8,128)(2,1)}, bf16[8,20,16,4096]{3,2,1,0:T(8,128)(2,1)}) custom-call(bf16[640,4096]{1,0:T(8,128)(2,1)} %tokens_ref.1, bf16[16,256,2048]{2,1,0:T(8,128)(2,1)} %bitcast.6, bf16[16,16,4096]{2,1,0:T(8,128)(2,1)} %bitcast.7, bf16[4,16,4096]{2,1,0:T(8,128)(2,1)} %reshape.65.up_ref, s32[640,256]{1,0:T(8,128)} %compare_select_fusion.code_ref), custom_call_target="tpu_custom_call" | custom-call | tf_op jit(solution)/shard_map/pallas_call | solution.py:380
  227.5 2.5 %copy.9 = bf16[640,1024]{1,0:T(8,128)(2,1)} copy(bf16[640,1024]{1,0:T(8,128)(2,1)} %get-tuple-element.6) | data formatting | bytes 2621440
  (1 shorter events, 0.0 us)

commit v4 on v3

--- a/solution.py
+++ b/solution.py
@@ -12,11 +12,11 @@
 FIRST = 3
 
 
-def chunks_of(down_slabs, slabs):
+def chunks_of(down_slabs):
     main = down_slabs - FIRST
     size = main // 3
     ranges = [(FIRST + i * size, size if i < 2 else main - 2 * size) for i in range(3)]
-    return ranges + [(down_slabs, slabs - down_slabs), (0, FIRST)]
+    return ranges + [(down_slabs, 0), (0, FIRST)]
 
 
 def kernel(
@@ -28,6 +28,7 @@
     code_ref,
     out_ref,
     buf,
+    up_buf,
     tok,
     tile,
     down_tile,
@@ -57,19 +58,24 @@
     partner = z * 2 + (1 - y)
     other = 1 - core
     down_slabs = down_ref.shape[0]
-    slabs = down_slabs + up_ref.shape[0]
+    up_at = down_slabs
     depth_slabs = weight_ref.shape[0]
     depth = down_ref.shape[2]
     slab = weight_ref.shape[1]
     tiles = weight_ref.shape[2] // slab
     half = tiles // 2
-    chunks = chunks_of(down_slabs, slabs)
+    chunks = chunks_of(down_slabs)
     main_count = len(chunks) - 1
 
     def mine(start, size):
         if start < down_slabs:
             return down_ref.at[pl.ds(start, size)]
-        return up_ref.at[pl.ds(start - down_slabs, size)]
+        return up_ref
+
+    def held(owner, start, size):
+        if start < down_slabs:
+            return buf.at[owner, pl.ds(start, size)]
+        return up_buf.at[owner]
 
 
     barrier = pltpu.get_barrier_semaphore()
@@ -91,14 +97,14 @@
         if chunk < len(chunks):
             start, size = chunks[chunk]
             owner = owner_z * 2 + y
-            source = mine(start, size) if step == 1 else buf.at[owner, pl.ds(start, size)]
+            source = mine(start, size) if step == 1 else held(owner, start, size)
         else:
             start, size = chunks[-1]
             owner = owner_z * 2 + (1 - y)
             source = buf.at[owner, pl.ds(start, size)]
         return pltpu.make_async_remote_copy(
             src_ref=source,
-            dst_ref=buf.at[owner, pl.ds(start, size)],
+            dst_ref=held(owner, start, size),
             send_sem=z_send.at[way, step - 1, chunk],
             recv_sem=z_recv.at[way, step - 1, chunk],
             device_id={"wide": me + 2 if way == 0 else me - 2},
@@ -108,8 +114,8 @@
     def y_copy(way, step, chunk, owner):
         start, size = chunks[chunk]
         return pltpu.make_async_remote_copy(
-            src_ref=buf.at[owner, pl.ds(start, size)],
-            dst_ref=buf.at[owner, pl.ds(start, size)],
+            src_ref=held(owner, start, size),
+            dst_ref=held(owner, start, size),
             send_sem=y_send.at[way, step - 1, chunk],
             recv_sem=y_recv.at[way, step - 1, chunk],
             device_id={"wide": partner},
@@ -120,11 +126,11 @@
         start, size = (
             (0, FIRST),
             (FIRST, down_slabs - FIRST),
-            (down_slabs, slabs - down_slabs),
+            (up_at, 0),
         )[which]
         return pltpu.make_async_remote_copy(
             src_ref=mine(start, size),
-            dst_ref=buf.at[owner, pl.ds(start, size)],
+            dst_ref=held(owner, start, size),
             send_sem=own_send.at[which],
             recv_sem=own_recv.at[which],
             device_id={"wide": partner},
@@ -228,29 +234,20 @@
         return lax.fori_loop(0, 4, body, zero)
 
     def shrink(down_source, up_source, owner):
-        groups = upv.shape[1]
-        width = upv.shape[4]
         down = pltpu.make_async_copy(down_source, down_tile, tile_sem.at[0])
         down.start()
-        ups = [
-            pltpu.make_async_copy(
-                up_source.at[:, :, pl.ds(g * width, width)], upv.at[owner, g], up_sem.at[g]
-            )
-            for g in range(groups)
-        ]
-        for up in ups:
-            up.start()
+        up = pltpu.make_async_copy(up_source, upv.at[owner], up_sem)
+        up.start()
         down.wait()
         total[...] += jnp.where(code_ref[...] == owner, down_product(), jnp.float32(0.0))
-        for up in ups:
-            up.wait()
+        up.wait()
 
     shrink(down_ref, up_ref, me)
 
     def arrived(owner):
         shrink(
             buf.at[owner, pl.ds(0, down_slabs)],
-            buf.at[owner, pl.ds(down_slabs, slabs - down_slabs)],
+            up_buf.at[owner],
             owner,
         )
 
@@ -308,7 +305,7 @@
 
     def finish(i, carry):
         columns = pl.ds(pl.multiple_of(i * slab, slab), slab)
-        right = upv[:, :, :, :, columns].reshape(wide_count * slab, slab)
+        right = upv[:, :, columns].reshape(wide_count * slab, slab)
         adapted = jnp.dot(spread[...], right, preferred_element_type=jnp.float32)
         value = part[half + i] + got[i] + adapted
         out_ref[:, columns] = value.astype(jnp.bfloat16)
@@ -354,10 +351,6 @@
     part_slabs = part // columns
     sub = 16
     down_slabs = columns // sub
-    groups = depth // part
-    up_rows = columns // groups
-    up_slabs = up_rows // sub
-    slabs = down_slabs + up_slabs
     planes = wide_count // 2
 
     up = lax.dynamic_slice_in_dim(adapter_up_weight, narrow_index * part, part, 2)
@@ -365,7 +358,7 @@
     kept = jnp.arange(rank_limit, dtype=jnp.int32)[None, :] < rank
     scale = jnp.where(kept, ALPHA / rank.astype(jnp.float32), jnp.float32(0.0))
     up = (up.astype(jnp.float32) * scale[:, :, None]).astype(jnp.bfloat16)
-    up = up.reshape(groups, up_rows, part).transpose(1, 0, 2).reshape(up_slabs, sub, depth)
+    up = up.reshape(columns, part)
     down = adapter_down_weight.transpose(1, 2, 0).reshape(down_slabs, sub, depth)
     column_adapter = jnp.arange(columns, dtype=jnp.int32) // rank_limit
     code = jnp.where(
@@ -377,27 +370,28 @@
     any_space = pl.BlockSpec(memory_space=pl.ANY)
     vmem = pl.BlockSpec(memory_space=pltpu.VMEM)
     dma = pltpu.SemaphoreType.DMA
-    out, _ = pl.pallas_call(
+    out, _, _ = pl.pallas_call(
         functools.partial(kernel, wide_count),
         out_shape=(
             jax.ShapeDtypeStruct((rows, part), jnp.bfloat16),
-            jax.ShapeDtypeStruct((wide_count, slabs, sub, depth), jnp.bfloat16),
+            jax.ShapeDtypeStruct((wide_count, down_slabs, sub, depth), jnp.bfloat16),
+            jax.ShapeDtypeStruct((wide_count, columns, part), jnp.bfloat16),
         ),
         in_specs=[any_space, any_space, any_space, any_space, vmem],
-        out_specs=(vmem, any_space),
+        out_specs=(vmem, any_space, any_space),
         scratch_shapes=[
             pltpu.VMEM((rows, depth), jnp.bfloat16),
             pltpu.VMEM((2, depth_slabs, columns, columns), jnp.bfloat16),
             pltpu.VMEM((down_slabs, sub, depth), jnp.bfloat16),
             pltpu.VMEM((2 * part_slabs, rows, columns), jnp.float32),
             pltpu.VMEM((part_slabs, rows, columns), jnp.float32),
-            pltpu.VMEM((wide_count, groups, up_slabs, sub, part), jnp.bfloat16),
+            pltpu.VMEM((wide_count, columns, part), jnp.bfloat16),
             pltpu.VMEM((rows, columns), jnp.float32),
             pltpu.VMEM((rows, columns), jnp.float32),
             pltpu.VMEM((rows, wide_count * columns), jnp.bfloat16),
             dma,
             dma((2,)),
-            dma((groups,)),
+            dma,
             dma((2, planes - 1, 6)),
             dma((2, planes - 1, 6)),
             dma((2, planes - 1, 4)),

time: 231 us -> 229 us (level)
  no operation moved by 1% of the time
where the time goes in v4:
time: 229 us; the launch traced here: 228 us
  Pallas kernels  221 us (97%)
  other arithmetic  5.19 us (2%)
  local copies, waits for them, and re-layouts  2.47 us (1%)
    pallas_call x1, Pallas kernels, local(): pl.pallas_call(functools.partial(kernel, wide_count), out_shape=(jax.Shap...  221 us

profile of v4, /device:TPU:1, one launch (start us, length us, event | category | flops | bytes accessed | tf_op | source)
XLA Modules:
  0.0 228.5 jit_solution(4055952918453658143)
XLA Ops:
  0.0 0.7 convert_divide_fusion
  0.7 0.7 fusion.2
  1.4 0.7 add_select_fusion.1
  2.1 2.0 multiply_convert_fusion
  4.1 1.1 compare_select_fusion.code_ref
  5.2 220.8 %shard_map.64 = (bf16[640,1024]{1,0:T(8,128)(2,1)}, bf16[8,16,16,4096]{3,2,1,0:T(8,128)(2,1)}, bf16[8,256,1024]{2,1,0:T(8,128)(2,1)}) custom-call(bf16[640,4096]{1,0:T(8,128)(2,1)} %tokens_ref.1, bf16[16,256,2048]{2,1,0:T(8,128)(2,1)} %bitcast.5, bf16[16,16,4096]{2,1,0:T(8,128)(2,1)} %bitcast.6, bf16[256,1024]{1,0:T(8,128)(2,1)} %bitcast.7, ...), custom_call_target="tpu_custom_call" | custom-call | tf_op jit(solution)/shard_map/pallas_call | solution.py:373
  226.0 2.5 %copy.8 = bf16[640,1024]{1,0:T(8,128)(2,1)} copy(bf16[640,1024]{1,0:T(8,128)(2,1)} %get-tuple-element.6) | data formatting | bytes 2621440
  (1 shorter events, 0.0 us)
